TPU v7x, 32 devices: a whole 2x2x4 slice. The times are simulated.
32 devices in a mesh: groups: 2 (over x), pages: 16 (over z, y, core).
Axes of the slice: x: 2, y: 2, z: 4, core: 2. Of those that a mesh axis runs over, the one named last changes fastest.
Arguments:
- queries: bfloat16 [2, 512, 8192], P(None, 'groups'), parts along dimension 1, may hold values from -14 to 14
- kv_cache: bfloat16 [256, 128, 2, 1024], P(('groups', 'pages')), parts along dimension 0, may hold values from -14 to 14
- w_out: bfloat16 [8192, 8192], P('pages'), may hold values from -0.0625 to 0.0625
- slot_page_before: int32 [256], P(('groups', 'pages')), parts along dimension 0, may hold values from -1 to 127, as said below
- slot_page_after: int32 [256], P(('groups', 'pages')), parts along dimension 0, may hold values from -1 to 127, as said below
- move_out: int32 [32, 4], P(('groups', 'pages')), parts along dimension 0, may hold values from -1 to 7, as said below
- move_in: int32 [32, 4], P(('groups', 'pages')), parts along dimension 0, may hold values from -1 to 7, as said below
- positions: int32 [2, 512], P(None, 'groups'), parts along dimension 1, may hold values from 0 to 16383, as said below
Outputs:
- attn_output: bfloat16 [2, 512, 8192], P(None, ('groups', 'pages')), parts along dimension 1
- cache_after: bfloat16 [256, 128, 2, 1024], P(('groups', 'pages')), parts along dimension 0
There are 2 independent parts, one for each index of `groups`. A program takes and returns all parts, laid end to end along the dimension named above; an argument that names none is the same for every part. Nothing has to cross between parts.
Inputs may be any that keep to these rules, and one draw needn't show every extreme that they name: `slot_page_before`: the logical page held by each slot; -1 marks a free slot; the live pages are the last ones of the sequence, numbered consecutively up to 127, each in exactly one slot; an owner's free slots are its last ones. `slot_page_after`: pages that are not sent keep their slot, each sent page sits in the slot that move_in names at its new owner, and a slot that sent its page is free. `move_out`: entry [j, o - 1] is a slot of owner j holding a live page, sent to owner (j + o) mod 16, or -1; the slots of one row differ; an owner sends at most one page to each of its next 4 owners. `move_in`: entry [j, o - 1] is a slot of owner j that is free before the moves, or -1, which it is exactly where move_out[(j - o) mod 16, o - 1] is -1; the slots of one row differ. Each row holds 256 consecutive positions; row 1 ends at the last position of the last live page; at most 256 positions lie between the end of row 0 and the start of row 1; all lie within the live pages.
All inputs are finite; a program needn't handle non-finite values.
Results may differ from a plain program's by a relative error of at most 0.0055.
Values may be sent and summed in bfloat16 or wider, within the bound.
A program may use at most 192 MiB of HBM per device.

v0:
```python
import jax
import jax.numpy as jnp
from jax import lax
from jax.sharding import PartitionSpec as P

HEADS = 64
KV_HEADS = 8
HEAD_DIM = 128
D = 8192
PAGE_TOK = 128
BLOCK = 256
MOVE_WIN = 4


floor_score = -1e30


def passed_along(block, axis, distance):
    devices = range(lax.axis_size(axis))
    route = [((i - distance) % len(devices), i) for i in devices]
    return lax.ppermute(block, axis, route)


def block_partials(query_rows, cache_rows, slot_table, positions_row):
    key_count = cache_rows.shape[0] * PAGE_TOK
    head_group = HEADS // KV_HEADS
    key_rows = cache_rows[:, :, 0, :].reshape(key_count, KV_HEADS, HEAD_DIM)
    value_rows = cache_rows[:, :, 1, :].reshape(key_count, KV_HEADS, HEAD_DIM)
    key_pos = (
        slot_table[:, None] * PAGE_TOK + jnp.arange(PAGE_TOK, dtype=jnp.int32)[None, :]
    ).reshape(key_count)
    live_keys = jnp.repeat(slot_table >= 0, PAGE_TOK)
    sub_rows = min(64, BLOCK)
    score_scale = HEAD_DIM ** (-0.5)
    queries_in = query_rows.reshape(BLOCK // sub_rows, sub_rows, KV_HEADS, head_group, HEAD_DIM)
    places = positions_row.reshape(BLOCK // sub_rows, sub_rows)

    def one_block(inputs):
        query_block, query_pos = inputs
        scores = (
            jnp.einsum("qhgd,khd->qhgk", query_block, key_rows, preferred_element_type=jnp.float32)
            * score_scale
        )
        visible = (live_keys[None, :] & (key_pos[None, :] <= query_pos[:, None]))[:, None, None, :]
        scores = jnp.where(visible, scores, floor_score)
        row_max = jnp.max(scores, axis=-1)
        weights = jnp.where(visible, jnp.exp(scores - row_max[..., None]), 0.0).astype(jnp.bfloat16)
        row_sum = jnp.sum(weights, axis=-1, dtype=jnp.float32)
        mixed_rows = jnp.einsum(
            "qhgk,khd->qhgd", weights, value_rows, preferred_element_type=jnp.float32
        )
        return (
            mixed_rows.reshape(sub_rows, HEADS * HEAD_DIM),
            row_max.reshape(sub_rows, HEADS),
            row_sum.reshape(sub_rows, HEADS),
        )

    mixed_rows, row_max, row_sum = lax.map(one_block, (queries_in, places))
    return (
        mixed_rows.reshape(BLOCK, HEADS * HEAD_DIM),
        row_max.reshape(BLOCK, HEADS),
        row_sum.reshape(BLOCK, HEADS),
    )


def combine_parts(part_out, part_max, part_sum):
    sources, item_count, head_count = part_max.shape
    part_out = part_out.reshape(sources, item_count, head_count, HEAD_DIM)
    overall = jnp.max(part_max, axis=0)
    factor = jnp.exp(part_max - overall[None])
    weighted = jnp.sum(factor[..., None] * part_out, axis=0)
    normalizer = jnp.sum(factor * part_sum, axis=0)
    return (
        (weighted / normalizer[..., None])
        .reshape(item_count, head_count * HEAD_DIM)
        .astype(jnp.bfloat16)
    )


def migrate_pages(kv_cache, slot_page_after, move_out, move_in):
    slot_ids = jnp.arange(kv_cache.shape[0], dtype=jnp.int32)
    arranged = jnp.where(
        (slot_page_after >= 0)[:, None, None, None], kv_cache, jnp.zeros((), kv_cache.dtype)
    )
    outgoing = kv_cache[jnp.maximum(move_out[0], 0)]
    for offset in range(1, MOVE_WIN + 1):
        arrived = passed_along(outgoing[offset - 1], "pages", offset)
        landing = (slot_ids == move_in[0, offset - 1])[:, None, None, None]
        arranged = jnp.where(landing, arrived[None], arranged)
    return arranged


def local(
    queries, kv_cache, w_out, slot_page_before, slot_page_after, move_out, move_in, positions
):
    owners = lax.axis_size("pages")
    tok_rows = BLOCK // owners
    cache_after = migrate_pages(kv_cache, slot_page_after, move_out, move_in)
    results = []
    for block_index, (cache_rows, slot_table) in enumerate(
        ((kv_cache, slot_page_before), (cache_after, slot_page_after))
    ):
        part_out, part_max, part_sum = block_partials(
            queries[block_index], cache_rows, slot_table, positions[block_index]
        )
        merged = combine_parts(
            lax.all_to_all(
                part_out.reshape(1, owners, tok_rows, D),
                "pages",
                split_axis=1,
                concat_axis=0,
                tiled=True,
            )[:, 0],
            lax.all_to_all(
                part_max.reshape(1, owners, tok_rows, HEADS),
                "pages",
                split_axis=1,
                concat_axis=0,
                tiled=True,
            )[:, 0],
            lax.all_to_all(
                part_sum.reshape(1, owners, tok_rows, HEADS),
                "pages",
                split_axis=1,
                concat_axis=0,
                tiled=True,
            )[:, 0],
        )
        attended = lax.all_to_all(merged, "pages", split_axis=1, concat_axis=0, tiled=True)
        results.append(
            lax.psum_scatter(
                jnp.dot(attended, w_out, preferred_element_type=jnp.float32),
                "pages",
                scatter_dimension=0,
                tiled=True,
            ).astype(jnp.bfloat16)
        )
    return (jnp.stack(results), cache_after)


def solution(mesh):
    in_specs = (
        P(None, "groups", None),
        P(("groups", "pages"), None, None, None),
        P("pages", None),
        P(("groups", "pages")),
        P(("groups", "pages")),
        P(("groups", "pages"), None),
        P(("groups", "pages"), None),
        P(None, "groups"),
    )
    out_specs = (P(None, ("groups", "pages"), None), P(("groups", "pages"), None, None, None))
    return jax.shard_map(local, mesh=mesh, in_specs=in_specs, out_specs=out_specs, check_vma=False)
```

profile of v0, /device:TPU:0, one launch (start us, length us, event | category | flops | bytes accessed | tf_op | source)
XLA Modules:
  0.0 818.6 jit_solution(12786084088419435648)
XLA Ops:
  7.8 7.1 gather_fusion
  23.2 18.6 %slice_reduce_fusion.2 = (bf16[8,128,1024]{2,1,0:T(8,128)(2,1)S(1)}, bf16[8,128,1024]{2,1,0:T(8,128)(2,1)}) fusion(bf16[8,128,2,1024]{3,2,1,0:T(2,128)(2,1)S(1)} %copy-done.2), kind=kLoop, calls=%fused_computation.59 | loop fusion | bytes 8388608 | tf_op jit(solution)/shard_map/slice | solution.py:28
  59.0 126.6 %while.30 = (s32[]{:T(128)}, f32[4,64,8192]{2,1,0:T(8,128)}, f32[4,64,64]{2,1,0:T(8,128)S(1)}, f32[4,64,64]{2,1,0:T(8,128)S(1)}, s32[4,64]{1,0:T(4,128)S(1)}, /*...) while((s32[]{:T(128)}, f32[4,64,8192]{2,1,0:T(8,128)}, ...), condition=%wide.region_3.4_spmd.clone, body=%wide.region_0.3_spmd.clone.sunk | while | flops 2210522112 | bytes 137965520 | solution.py:58
  64.8 5.7 copy-done
  70.5 6.1 convert_reduce_fusion.4
  77.0 8.9 %fusion.58 = f32[64,8,8,128]{3,2,0,1:T(8,128)S(1)} fusion(bf16[1024,8,128]{2,0,1:T(8,128)(2,1)} %get-tuple-element.508, f32[8,64,8,1024]{3,2,1,0:T(8,128)} %copy-done, f32[64,8,8]{2,0,1:T(8,128)S(1)} %get-tuple-element.429, pred[64,1024]{1,0:T(8,128)(4,1)S(1)} %compare_and_fusion.4), kind=kOutput, calls=%fused_computation.16.clone.1 | convolution fusion | flops 1094713344 | bytes 21053440 | tf_op jit(solution)/shard_map/while/body/eval_jaxpr/qhgk,khd->qhgd/dot_general | solution.py:49
  91.1 5.2 bitcast_reduce_fusion.6
  96.4 5.7 copy-done
  102.1 6.1 convert_reduce_fusion.4
  108.6 8.9 %fusion.58 = f32[64,8,8,128]{3,2,0,1:T(8,128)S(1)} fusion(bf16[1024,8,128]{2,0,1:T(8,128)(2,1)} %get-tuple-element.508, f32[8,64,8,1024]{3,2,1,0:T(8,128)} %copy-done, f32[64,8,8]{2,0,1:T(8,128)S(1)} %get-tuple-element.429, pred[64,1024]{1,0:T(8,128)(4,1)S(1)} %compare_and_fusion.4), kind=kOutput, calls=%fused_computation.16.clone.1 | convolution fusion | flops 1094713344 | bytes 21053440 | tf_op jit(solution)/shard_map/while/body/eval_jaxpr/qhgk,khd->qhgd/dot_general | solution.py:49
  122.7 5.2 bitcast_reduce_fusion.6
  127.9 5.7 copy-done
  133.6 6.1 convert_reduce_fusion.4
  140.2 8.9 %fusion.58 = f32[64,8,8,128]{3,2,0,1:T(8,128)S(1)} fusion(bf16[1024,8,128]{2,0,1:T(8,128)(2,1)} %get-tuple-element.508, f32[8,64,8,1024]{3,2,1,0:T(8,128)} %copy-done, f32[64,8,8]{2,0,1:T(8,128)S(1)} %get-tuple-element.429, pred[64,1024]{1,0:T(8,128)(4,1)S(1)} %compare_and_fusion.4), kind=kOutput, calls=%fused_computation.16.clone.1 | convolution fusion | flops 1094713344 | bytes 21053440 | tf_op jit(solution)/shard_map/while/body/eval_jaxpr/qhgk,khd->qhgd/dot_general | solution.py:49
  159.6 5.7 copy-done
  165.3 6.1 convert_reduce_fusion.4
  171.8 8.9 %fusion.58 = f32[64,8,8,128]{3,2,0,1:T(8,128)S(1)} fusion(bf16[1024,8,128]{2,0,1:T(8,128)(2,1)} %get-tuple-element.508, f32[8,64,8,1024]{3,2,1,0:T(8,128)} %copy-done, f32[64,8,8]{2,0,1:T(8,128)S(1)} %get-tuple-element.429, pred[64,1024]{1,0:T(8,128)(4,1)S(1)} %compare_and_fusion.4), kind=kOutput, calls=%fused_computation.16.clone.1 | convolution fusion | flops 1094713344 | bytes 21053440 | tf_op jit(solution)/shard_map/while/body/eval_jaxpr/qhgk,khd->qhgd/dot_general | solution.py:49
  192.9 5.5 all-to-all-done
  203.2 5.4 copy.84
  211.3 6.3 all-to-all-start.1
  223.0 9.4 %mul.54 = f32[1,16,16,8192]{3,2,0,1:T(8,128)} reshape(f32[16,16,64,128]{3,2,1,0:T(8,128)} %mul.53) | data formatting | bytes 16777216 | tf_op jit(solution)/shard_map/mul | solution.py:71
  232.7 9.4 %broadcast_select_fusion.4 = bf16[8,128,2,1024]{3,2,1,0:T(2,128)(2,1)S(1)} fusion(pred[8]{0:T(512)(128)(4,1)S(1)} %get-tuple-element.307, pred[8]{0:T(512)(128)(4,1)S(1)} %get-tuple-element.306, pred[8]{0:T(512)(128)(4,1)S(1)} %get-tuple-element.305, pred[8]{0:T(512)(128)(4,1)S(1)} %get-tuple-element.304, bf16[8,128,2,1024]{3,2,1,0:T(2,128)(2,1)} %param.13, ...), kind=kLoop, calls=%fused_computation.55 | loop fusion | flops 10485760 | bytes 10485800 | tf_op jit(solution)/shard_map/jit(_where)/select_n | solution.py:89
  242.2 18.6 %slice_reduce_fusion = (bf16[8,128,1024]{2,1,0:T(8,128)(2,1)S(1)}, bf16[8,128,1024]{2,1,0:T(8,128)(2,1)}) fusion(bf16[8,128,2,1024]{3,2,1,0:T(2,128)(2,1)S(1)} %broadcast_select_fusion.4), kind=kLoop, calls=%fused_computation.56 | loop fusion | bytes 8388608 | tf_op jit(solution)/shard_map/slice | solution.py:28
  271.1 126.6 %while.31 = (s32[]{:T(128)}, f32[4,64,8192]{2,1,0:T(8,128)}, f32[4,64,64]{2,1,0:T(8,128)S(1)}, f32[4,64,64]{2,1,0:T(8,128)S(1)}, s32[4,64]{1,0:T(4,128)S(1)}, /*...) while((s32[]{:T(128)}, f32[4,64,8192]{2,1,0:T(8,128)}, ...), condition=%wide.region_11.12_spmd.clone, body=%wide.region_8.11_spmd.clone.sunk | while | flops 2210522112 | bytes 137965520 | solution.py:58
  276.9 5.7 copy-done.1
  282.6 6.1 convert_reduce_fusion.5
  289.1 8.9 %fusion.62 = f32[64,8,8,128]{3,2,0,1:T(8,128)S(1)} fusion(bf16[1024,8,128]{2,0,1:T(8,128)(2,1)} %get-tuple-element.475, f32[8,64,8,1024]{3,2,1,0:T(8,128)} %copy-done.1, f32[64,8,8]{2,0,1:T(8,128)S(1)} %get-tuple-element.443, pred[64,1024]{1,0:T(8,128)(4,1)S(1)} %compare_and_fusion.5), kind=kOutput, calls=%fused_computation.38.clone.1 | convolution fusion | flops 1094713344 | bytes 21053440 | tf_op jit(solution)/shard_map/while/body/eval_jaxpr/qhgk,khd->qhgd/dot_general | solution.py:49
  308.5 5.7 copy-done.1
  314.2 6.1 convert_reduce_fusion.5
  320.7 8.9 %fusion.62 = f32[64,8,8,128]{3,2,0,1:T(8,128)S(1)} fusion(bf16[1024,8,128]{2,0,1:T(8,128)(2,1)} %get-tuple-element.475, f32[8,64,8,1024]{3,2,1,0:T(8,128)} %copy-done.1, f32[64,8,8]{2,0,1:T(8,128)S(1)} %get-tuple-element.443, pred[64,1024]{1,0:T(8,128)(4,1)S(1)} %compare_and_fusion.5), kind=kOutput, calls=%fused_computation.38.clone.1 | convolution fusion | flops 1094713344 | bytes 21053440 | tf_op jit(solution)/shard_map/while/body/eval_jaxpr/qhgk,khd->qhgd/dot_general | solution.py:49
  340.1 5.7 copy-done.1
  345.8 6.1 convert_reduce_fusion.5
  352.4 8.9 %fusion.62 = f32[64,8,8,128]{3,2,0,1:T(8,128)S(1)} fusion(bf16[1024,8,128]{2,0,1:T(8,128)(2,1)} %get-tuple-element.475, f32[8,64,8,1024]{3,2,1,0:T(8,128)} %copy-done.1, f32[64,8,8]{2,0,1:T(8,128)S(1)} %get-tuple-element.443, pred[64,1024]{1,0:T(8,128)(4,1)S(1)} %compare_and_fusion.5), kind=kOutput, calls=%fused_computation.38.clone.1 | convolution fusion | flops 1094713344 | bytes 21053440 | tf_op jit(solution)/shard_map/while/body/eval_jaxpr/qhgk,khd->qhgd/dot_general | solution.py:49
  371.7 5.7 copy-done.1
  377.4 6.1 convert_reduce_fusion.5
  383.9 8.9 %fusion.62 = f32[64,8,8,128]{3,2,0,1:T(8,128)S(1)} fusion(bf16[1024,8,128]{2,0,1:T(8,128)(2,1)} %get-tuple-element.475, f32[8,64,8,1024]{3,2,1,0:T(8,128)} %copy-done.1, f32[64,8,8]{2,0,1:T(8,128)S(1)} %get-tuple-element.443, pred[64,1024]{1,0:T(8,128)(4,1)S(1)} %compare_and_fusion.5), kind=kOutput, calls=%fused_computation.38.clone.1 | convolution fusion | flops 1094713344 | bytes 21053440 | tf_op jit(solution)/shard_map/while/body/eval_jaxpr/qhgk,khd->qhgd/dot_general | solution.py:49
  399.2 6.1 all-to-all-start.4
  405.3 6.6 multiply_reduce_fusion.1
  412.3 6.0 all-to-all-start.6
  418.5 6.6 all-to-all-done.6
  425.2 12.6 %all_to_all.86 = bf16[16,16,512]{2,0,1:T(8,128)(2,1)S(1)} all-to-all(bf16[16,16,512]{2,0,1:T(8,128)(2,1)S(1)} %copy.53), channel_id=1, replica_groups=mesh['groups'=2,'pages'=16] {'pages'}, dimensions={1} | all-to-all | bytes 524288 | tf_op jit(solution)/shard_map/all_to_all | solution.py:129
  442.7 9.0 %fusion.41 = f32[256,8192]{1,0:T(8,128)} fusion(bf16[256,512]{1,0:T(8,128)(2,1)S(1)} %bitcast.262, bf16[512,8192]{1,0:T(8,128)(2,1)} %param.14), kind=kOutput, calls=%fused_computation.96 | convolution fusion | flops 2147483648 | bytes 17039360 | tf_op jit(solution)/shard_map/dot_general | solution.py:132
  458.3 9.7 %mul.59 = f32[1,16,16,8192]{3,2,0,1:T(8,128)} reshape(f32[16,16,64,128]{3,2,1,0:T(8,128)} %mul.58) | data formatting | bytes 16777216 | tf_op jit(solution)/shard_map/mul | solution.py:71
  468.3 158.7 %all-to-all-done.5 = f32[1,16,16,8192]{3,2,0,1:T(8,128)} async-done(((f32[1,16,16,8192]{3,2,0,1:T(8,128)}), f32[1,16,16,8192]{3,2,0,1:T(8,128)}, u32[]{:S(2)}, u32[]{:S(2)}) %all-to-all-start.5) | async-done | bytes 8388640 | tf_op jit(solution)/shard_map/all_to_all | solution.py:107
  627.0 7.0 multiply_reduce_fusion
  634.5 62.7 %all_to_all.87 = bf16[16,16,512]{2,0,1:T(8,128)(2,1)S(1)} all-to-all(bf16[16,16,512]{2,0,1:T(8,128)(2,1)S(1)} %copy.61), channel_id=1, replica_groups=mesh['groups'=2,'pages'=16] {'pages'}, dimensions={1} | all-to-all | bytes 524288 | tf_op jit(solution)/shard_map/all_to_all | solution.py:129
  697.3 9.0 %fusion.42 = f32[256,8192]{1,0:T(8,128)} fusion(bf16[256,512]{1,0:T(8,128)(2,1)S(1)} %bitcast.263, bf16[512,8192]{1,0:T(8,128)(2,1)} %param.14), kind=kOutput, calls=%fused_computation.97 | convolution fusion | flops 2147483648 | bytes 17039360 | tf_op jit(solution)/shard_map/dot_general | solution.py:132
  707.5 101.9 %reduce-scatter.5.cloned.1.call-done = f32[16,8192]{1,0:T(8,128)} async-done(((f32[256,8192]{1,0:T(8,128)}), f32[16,8192]{1,0:T(8,128)}) %reduce-scatter.5.cloned.1.call-update) | async-done | bytes 524304 | tf_op jit(solution)/shard_map/reduce_scatter | solution.py:131
  (204 shorter events, 149.9 us)
Async XLA Ops:
  14.9 8.3 %copy-start.2 = (bf16[8,128,2,1024]{3,2,1,0:T(2,128)(2,1)S(1)}, bf16[8,128,2,1024]{3,2,1,0:T(2,128)(2,1)}, u32[]{:S(2)}) copy-start(bf16[8,128,2,1024]{3,2,1,0:T(2,128)(2,1)} %param.13) | copy-start | bytes 12582916
  14.9 26.9 %copy-start.7 = (s32[8]{0:T(128)S(1)}, s32[8]{0:T(128)}, u32[]{:S(2)}) copy-start(s32[8]{0:T(128)} %param.15) | copy-start | bytes 100
  17.3 215.4 %collective-permute-start = (bf16[128,2,1024]{2,1,0:T(2,128)(2,1)}, bf16[128,2,1024]{2,1,0:T(2,128)(2,1)}, u32[]{:S(2)}, u32[]{:S(2)}) collective-permute-start(bf16[128,2,1024]{2,1,0:T(2,128)(2,1)} %get-tuple-element.296), channel_id=1, source_target_pairs={{12,0},{13,1},{14,2},{15,3},{0,4},{1,5},{2,6},{3,7},{4,8},{5,9},{6... | collective-permute-start | bytes 1572872 | tf_op jit(solution)/shard_map/ppermute | solution.py:21
  20.3 212.4 %collective-permute-start.1 = (bf16[128,2,1024]{2,1,0:T(2,128)(2,1)}, bf16[128,2,1024]{2,1,0:T(2,128)(2,1)}, u32[]{:S(2)}, u32[]{:S(2)}) collective-permute-start(bf16[128,2,1024]{2,1,0:T(2,128)(2,1)} %get-tuple-element.298), channel_id=1, source_target_pairs={{13,0},{14,1},{15,2},{0,3},{1,4},{2,5},{3,6},{4,7},{5,8},{6,9},{7,... | collective-permute-start | bytes 1572872 | tf_op jit(solution)/shard_map/ppermute | solution.py:21
  21.0 211.7 %collective-permute-start.2 = (bf16[128,2,1024]{2,1,0:T(2,128)(2,1)}, bf16[128,2,1024]{2,1,0:T(2,128)(2,1)}, u32[]{:S(2)}, u32[]{:S(2)}) collective-permute-start(bf16[128,2,1024]{2,1,0:T(2,128)(2,1)} %get-tuple-element.297), channel_id=1, source_target_pairs={{14,0},{15,1},{0,2},{1,3},{2,4},{3,5},{4,6},{5,7},{6,8},{7,9},{8,1... | collective-permute-start | bytes 1572872 | tf_op jit(solution)/shard_map/ppermute | solution.py:21
  22.5 210.2 %collective-permute-start.3 = (bf16[128,2,1024]{2,1,0:T(2,128)(2,1)}, bf16[128,2,1024]{2,1,0:T(2,128)(2,1)}, u32[]{:S(2)}, u32[]{:S(2)}) collective-permute-start(bf16[128,2,1024]{2,1,0:T(2,128)(2,1)} %get-tuple-element.299), channel_id=1, source_target_pairs={{15,0},{0,1},{1,2},{2,3},{3,4},{4,5},{5,6},{6,7},{7,8},{8,9},{9,10... | collective-permute-start | bytes 1572872 | tf_op jit(solution)/shard_map/ppermute | solution.py:21
  41.8 5.1 copy-start.6
  47.0 3.1 copy-start.4
  59.0 132.5 %copy-start.8 = (s32[8]{0:T(128)S(1)}, s32[8]{0:T(128)}, u32[]{:S(2)}) copy-start(s32[8]{0:T(128)} %param.16) | copy-start | bytes 100
  59.0 133.2 %copy-start.5 = (s32[1,4]{1,0:T(1,128)S(1)}, s32[1,4]{1,0:T(1,128)}, u32[]{:S(2)}) copy-start(s32[1,4]{1,0:T(1,128)} %param.18) | copy-start | bytes 52
  64.7 5.7 copy-start
  96.4 5.7 copy-start
  127.9 5.7 copy-start
  159.5 5.7 copy-start
  186.4 12.0 %all-to-all-start = ((f32[16,1,1024]{2,1,0:T(1,128)}), f32[16,1,1024]{2,1,0:T(1,128)S(1)}, u32[]{:S(2)}, u32[]{:S(2)}) async-start(f32[16,1,1024]{2,1,0:T(1,128)} %reshape.268), calls=%async_computation | async-start | bytes 131072 | tf_op jit(solution)/shard_map/all_to_all | solution.py:114
  198.4 12.9 %all-to-all-start.2 = ((f32[16,1,1024]{2,1,0:T(1,128)}), f32[16,1,1024]{2,1,0:T(1,128)S(1)}, u32[]{:S(2)}, u32[]{:S(2)}) async-start(f32[16,1,1024]{2,1,0:T(1,128)} %reshape.270), calls=%async_computation.2 | async-start | bytes 131072 | tf_op jit(solution)/shard_map/all_to_all | solution.py:121
  211.3 187.9 %all-to-all-start.1 = ((f32[1,16,16,8192]{3,2,0,1:T(8,128)}), f32[1,16,16,8192]{3,2,0,1:T(8,128)}, u32[]{:S(2)}, u32[]{:S(2)}) async-start(f32[1,16,16,8192]{3,2,0,1:T(8,128)} %bitcast.245), calls=%async_computation.1 | async-start | bytes 16777216 | tf_op jit(solution)/shard_map/all_to_all | solution.py:107
  242.2 20.8 %copy-start.3 = (bf16[8,128,2,1024]{3,2,1,0:T(2,128)(2,1)}, bf16[8,128,2,1024]{3,2,1,0:T(2,128)(2,1)S(1)}, u32[]{:S(2)}) copy-start(bf16[8,128,2,1024]{3,2,1,0:T(2,128)(2,1)S(1)} %broadcast_select_fusion.4) | copy-start | bytes 12582916
  276.9 5.7 copy-start.1
  308.5 5.7 copy-start.1
  340.1 5.7 copy-start.1
  371.7 5.7 copy-start.1
  399.2 13.0 %all-to-all-start.4 = ((f32[16,1,1024]{2,1,0:T(1,128)}), f32[16,1,1024]{2,1,0:T(1,128)S(1)}, u32[]{:S(2)}, u32[]{:S(2)}) async-start(f32[16,1,1024]{2,1,0:T(1,128)} %reshape.264), calls=%async_computation.5 | async-start | bytes 131072 | tf_op jit(solution)/shard_map/all_to_all | solution.py:114
  412.3 12.9 %all-to-all-start.6 = ((f32[16,1,1024]{2,1,0:T(1,128)}), f32[16,1,1024]{2,1,0:T(1,128)S(1)}, u32[]{:S(2)}, u32[]{:S(2)}) async-start(f32[16,1,1024]{2,1,0:T(1,128)} %reshape.266), calls=%async_computation.7 | async-start | bytes 131072 | tf_op jit(solution)/shard_map/all_to_all | solution.py:121
  437.8 189.2 %all-to-all-start.5 = ((f32[1,16,16,8192]{3,2,0,1:T(8,128)}), f32[1,16,16,8192]{3,2,0,1:T(8,128)}, u32[]{:S(2)}, u32[]{:S(2)}) async-start(f32[1,16,16,8192]{3,2,0,1:T(8,128)} %bitcast.244), calls=%async_computation.6 | async-start | bytes 16777216 | tf_op jit(solution)/shard_map/all_to_all | solution.py:107
  442.6 263.7 %reduce-scatter.3.cloned.1.call-start = ((), (), s32[]{:S(2)}) async-start(), calls=%async_computation.10 | async-start | bytes 8912896 | tf_op jit(solution)/shard_map/reduce_scatter | solution.py:131
  451.7 357.7 %reduce-scatter.5.cloned.1.call-start = ((), (), s32[]{:S(2)}) async-start(), calls=%async_computation.11 | async-start | bytes 8912896 | tf_op jit(solution)/shard_map/reduce_scatter | solution.py:131
Sparse Core Ops, SparseCore 0:
  451.8 206.0 reduce-scatter.2
  706.5 102.8 reduce-scatter.4
where the time goes:
time: 827 us; the launch traced here: 819 us
  waiting for transfers between devices  273 us (33%)
  local copies, waits for them, and re-layouts  203 us (25%)
  matrix products  131 us (16%)
  other arithmetic  82.8 us (10%)
  blocking collectives  75.4 us (9%)
  starting transfers between devices  37.8 us (5%)
  between operations  15 us (2%)
    all_to_all x2, waiting for transfers between devices, local(): lax.all_to_all(part_out.reshape(1, owners, tok_rows, D), 'pages', split_a...  159 us
    reduce_scatter x2, waiting for transfers between devices, local(): lax.psum_scatter(jnp.dot(attended, w_out, preferred_element_type=jnp.floa...  102 us
    all_to_all x2, blocking collectives, local(): lax.all_to_all(merged, 'pages', split_axis=1, concat_axis=0, tiled=True)  75.4 us
    dot_general x8, matrix products, one_block(): jnp.einsum('qhgk,khd->qhgd', weights, value_rows, preferred_element_type=...  71.5 us
    reduce_sum x8, other arithmetic, one_block(): row_sum = jnp.sum(weights, axis=-1, dtype=jnp.float32)  49 us
    while x16, local copies, waits for them, and re-layouts  45.6 us
    dot_general x8, matrix products, one_block(): jnp.einsum('qhgd,khd->qhgk', query_block, key_rows, preferred_element_typ...  41.9 us
    slice x2, local copies, waits for them, and re-layouts, block_partials(): value_rows = cache_rows[:, :, 1, :].reshape(key_count, KV_HEADS, HEAD_DIM)  37.2 us
  transfers between devices with their start and end apart: 12, of which 4 were waited for; matrix products, arithmetic and copies ran while one was open for 44% of the time, Pallas kernels for 0%

commit v1 on v0

v1 whole, which is shorter than its diff:
```python
import functools
import math

import jax
import jax.numpy as jnp
from jax import lax
from jax.experimental import pallas as pl
from jax.experimental.pallas import tpu as pltpu
from jax.sharding import PartitionSpec as P

HEADS = 64
KV_HEADS = 8
HEAD_DIM = 128
PAGE_TOK = 128
MOVE_WIN = 4
SUM_ROWS = 16

floor_score = -1e30


def bit_of(me, stage):
    return lax.rem(me // (1 << stage), 2)


def partner_of(me, stage):
    return me + (1 << stage) * (1 - 2 * bit_of(me, stage))


def greet_partners(me, stages):
    barrier = pltpu.get_barrier_semaphore()
    for s in range(stages):
        pl.semaphore_signal(
            barrier, inc=1, device_id={"pages": partner_of(me, s)}, device_id_type=pl.DeviceIdType.MESH
        )
    pl.semaphore_wait(barrier, stages)


def to_partner(me, stage, src, dst, send_sem, recv_sem):
    return pltpu.make_async_remote_copy(
        src_ref=src,
        dst_ref=dst,
        send_sem=send_sem,
        recv_sem=recv_sem,
        device_id={"pages": partner_of(me, stage)},
        device_id_type=pl.DeviceIdType.MESH,
    )


def halving_schedule(chunks, stages, lag, produce, start, merge):
    def step(t, carry):
        @pl.when(t < chunks)
        def _():
            produce(t)
            start(0, t)

        for s in reversed(range(stages)):
            i = t - 1 - lag * s

            @pl.when((i >= 0) & (i < chunks))
            def _():
                merge(s, i)
                if s + 1 < stages:
                    start(s + 1, i)

        return carry

    lax.fori_loop(0, chunks + 1 + lag * (stages - 1), step, 0)


def attention_kernel(n, slots, q_ref, k_ref, vt_ref, bias_ref, out_ref, *scratch):
    stages = n.bit_length() - 1
    keep, keep_l, send, send_l, recv, recv_l = (
        scratch[k * stages : (k + 1) * stages] for k in range(6)
    )
    sems = scratch[6 * stages]
    me = lax.axis_index("pages")
    own_heads = HEADS // n
    tokens = q_ref.shape[1]
    chunks = 2 * own_heads
    group = HEADS // KV_HEADS
    score_scale = HEAD_DIM ** (-0.5) * math.log2(math.e)
    greet_partners(me, stages)

    def copies(s, i):
        return (
            to_partner(me, s, send[s].at[i], recv[s].at[i], sems.at[0, s, i], sems.at[1, s, i]),
            to_partner(me, s, send_l[s].at[i], recv_l[s].at[i], sems.at[2, s, i], sems.at[3, s, i]),
        )

    def start(s, i):
        for copy in copies(s, i):
            copy.start()

    def produce(i):
        block, j = i // own_heads, lax.rem(i, own_heads)
        mine = bit_of(me, 0)
        slot = lax.rem(i, slots)

        def pair(r, carry):
            for sent in (True, False):
                owner = 2 * r + (1 - mine if sent else mine)
                head = owner * own_heads + j
                kv = head // group
                keys = k_ref[:, pl.ds(pl.multiple_of(kv * HEAD_DIM, HEAD_DIM), HEAD_DIM)]
                rows = q_ref[block, :, pl.ds(pl.multiple_of(head * HEAD_DIM, HEAD_DIM), HEAD_DIM)]
                scores = lax.dot_general(
                    keys, rows, (((1,), (1,)), ((), ())), preferred_element_type=jnp.float32
                )
                scores = scores * score_scale + bias_ref[block]
                top = jnp.max(scores, axis=0, keepdims=True)
                weights = jnp.exp2(scores - top).astype(jnp.bfloat16)
                mixed = jnp.dot(vt_ref[kv], weights, preferred_element_type=jnp.float32)
                total = mixed[HEAD_DIM : HEAD_DIM + 1]
                mixed = mixed[:HEAD_DIM] / total
                level = top + jnp.log2(total)
                if sent:
                    send[0][i, r] = mixed.astype(jnp.bfloat16)
                    send_l[0][i, pl.ds(r, 1)] = level
                else:
                    keep[0][slot, r] = mixed
                    keep_l[0][slot, pl.ds(r, 1)] = level
            return carry

        lax.fori_loop(0, n // 2, pair, 0)

    def merge(s, i):
        for copy in copies(s, i):
            copy.wait_recv()
        slot = lax.rem(i, slots)

        def merged(r):
            la, lb = keep_l[s][slot, pl.ds(r, 1)], recv_l[s][i, pl.ds(r, 1)]
            top = jnp.maximum(la, lb)
            ea, eb = jnp.exp2(la - top), jnp.exp2(lb - top)
            total = ea + eb
            mixed = keep[s][slot, r] * (ea / total) + recv[s][i, r].astype(jnp.float32) * (eb / total)
            return mixed, top + jnp.log2(total)

        if s + 1 == stages:
            mixed, _ = merged(0)
            block, j = i // own_heads, lax.rem(i, own_heads)
            out_ref[
                pl.ds(pl.multiple_of(block * tokens, tokens), tokens),
                pl.ds(pl.multiple_of(j * HEAD_DIM, HEAD_DIM), HEAD_DIM),
            ] = mixed.T.astype(jnp.bfloat16)
            return
        mine = bit_of(me, s + 1)
        for r in range(n >> (s + 2)):
            mixed, level = merged(2 * r + 1 - mine)
            send[s + 1][i, r] = mixed.astype(jnp.bfloat16)
            send_l[s + 1][i, pl.ds(r, 1)] = level
            mixed, level = merged(2 * r + mine)
            keep[s + 1][slot, r] = mixed
            keep_l[s + 1][slot, pl.ds(r, 1)] = level

    halving_schedule(chunks, stages, 1, produce, start, merge)

    def finish(i, carry):
        for s in range(stages):
            for copy in copies(s, i):
                copy.wait_send()
        return carry

    lax.fori_loop(0, chunks, finish, 0)


def project_kernel(n, width, attended_ref, w_ref, out_ref, *scratch):
    stages = n.bit_length() - 1
    keep, send, recv = (scratch[k * stages : (k + 1) * stages] for k in range(3))
    product, sems = scratch[3 * stages :]
    me = lax.axis_index("pages")
    tok_rows = out_ref.shape[1]
    block_rows = attended_ref.shape[0] // 2
    chunks = w_ref.shape[1] // width
    greet_partners(me, stages)

    def copy(s, i):
        return to_partner(me, s, send[s].at[i], recv[s].at[i], sems.at[0, s, i], sems.at[1, s, i])

    def start(s, i):
        copy(s, i).start()

    def columns(i):
        return pl.ds(pl.multiple_of(i * width, width), width)

    def produce(i):
        product[...] = jnp.dot(
            attended_ref[...], w_ref[:, columns(i)], preferred_element_type=jnp.float32
        )
        mine = bit_of(me, 0)

        def owner_rows(owner):
            first = pl.multiple_of(owner * tok_rows, tok_rows)
            return jnp.concatenate(
                [product[pl.ds(first + block * block_rows, tok_rows)] for block in range(2)], axis=0
            )

        for r in range(n // 2):
            send[0][i, r] = owner_rows(2 * r + 1 - mine).astype(jnp.bfloat16)
            keep[0][i, r] = owner_rows(2 * r + mine)

    def merge(s, i):
        copy(s, i).wait_recv()

        def merged(r):
            return keep[s][i, r] + recv[s][i, r].astype(jnp.float32)

        if s + 1 == stages:
            rows = merged(0)
            for block in range(2):
                out_ref[block, :, columns(i)] = rows[block * tok_rows : (block + 1) * tok_rows].astype(
                    jnp.bfloat16
                )
            return
        mine = bit_of(me, s + 1)
        for r in range(n >> (s + 2)):
            send[s + 1][i, r] = merged(2 * r + 1 - mine).astype(jnp.bfloat16)
            keep[s + 1][i, r] = merged(2 * r + mine)

    halving_schedule(chunks, stages, 2, produce, start, merge)

    def finish(i, carry):
        for s in range(stages):
            copy(s, i).wait_send()
        return carry

    lax.fori_loop(0, chunks, finish, 0)


def attention(queries, keys, values_t, bias, n):
    tokens = queries.shape[1]
    own_heads = HEADS // n
    stages = n.bit_length() - 1
    chunks = 2 * own_heads
    slots = 2
    parts = [n >> (s + 1) for s in range(stages)]
    rows = [max(8, part) for part in parts]
    vmem = pl.BlockSpec(memory_space=pltpu.VMEM)
    key_count = keys.shape[0]
    return pl.pallas_call(
        functools.partial(attention_kernel, n, slots),
        out_shape=jax.ShapeDtypeStruct((2 * tokens, own_heads * HEAD_DIM), jnp.bfloat16),
        in_specs=[vmem] * 4,
        out_specs=vmem,
        scratch_shapes=[pltpu.VMEM((slots, p, HEAD_DIM, tokens), jnp.float32) for p in parts]
        + [pltpu.VMEM((slots, p, tokens), jnp.float32) for p in rows]
        + [pltpu.VMEM((chunks, p, HEAD_DIM, tokens), jnp.bfloat16) for p in parts]
        + [pltpu.VMEM((chunks, p, tokens), jnp.float32) for p in rows]
        + [pltpu.VMEM((chunks, p, HEAD_DIM, tokens), jnp.bfloat16) for p in parts]
        + [pltpu.VMEM((chunks, p, tokens), jnp.float32) for p in rows]
        + [pltpu.SemaphoreType.DMA((4, stages, chunks))],
        compiler_params=pltpu.CompilerParams(
            collective_id=0, has_side_effects=True, vmem_limit_bytes=60 * 1024 * 1024
        ),
        cost_estimate=pl.CostEstimate(
            flops=4 * 2 * tokens * HEADS * HEAD_DIM * key_count,
            bytes_accessed=queries.size * 2 + key_count * KV_HEADS * HEAD_DIM * 4,
            transcendentals=2 * tokens * HEADS * key_count,
        ),
    )(queries, keys, values_t, bias)


def project(attended, w_out, n):
    rows, depth = attended.shape
    d = w_out.shape[1]
    stages = n.bit_length() - 1
    width = d // 8
    chunks = d // width
    tile = rows // n
    parts = [n >> (s + 1) for s in range(stages)]
    vmem = pl.BlockSpec(memory_space=pltpu.VMEM)
    return pl.pallas_call(
        functools.partial(project_kernel, n, width),
        out_shape=jax.ShapeDtypeStruct((2, rows // 2 // n, d), jnp.bfloat16),
        in_specs=[vmem] * 2,
        out_specs=vmem,
        scratch_shapes=[pltpu.VMEM((chunks, p, tile, width), jnp.float32) for p in parts]
        + [pltpu.VMEM((chunks, p, tile, width), jnp.bfloat16) for p in parts] * 2
        + [pltpu.VMEM((rows, width), jnp.float32), pltpu.SemaphoreType.DMA((2, stages, chunks))],
        compiler_params=pltpu.CompilerParams(
            collective_id=1, has_side_effects=True, vmem_limit_bytes=60 * 1024 * 1024
        ),
        cost_estimate=pl.CostEstimate(
            flops=2 * rows * depth * d, bytes_accessed=depth * d * 2, transcendentals=0
        ),
    )(attended, w_out)


def passed_along(block, axis, distance):
    devices = range(lax.axis_size(axis))
    route = [((i - distance) % len(devices), i) for i in devices]
    return lax.ppermute(block, axis, route)


def migrate_pages(kv_cache, slot_page_after, move_out, move_in):
    slot_ids = jnp.arange(kv_cache.shape[0], dtype=jnp.int32)
    arranged = jnp.where(
        (slot_page_after >= 0)[:, None, None, None], kv_cache, jnp.zeros((), kv_cache.dtype)
    )
    for offset in range(1, MOVE_WIN + 1):
        outgoing = lax.dynamic_index_in_dim(
            kv_cache, jnp.maximum(move_out[0, offset - 1], 0), 0, keepdims=False
        )
        arrived = passed_along(outgoing, "pages", offset)
        landing = (slot_ids == move_in[0, offset - 1])[:, None, None, None]
        arranged = jnp.where(landing, arrived[None], arranged)
    return arranged


def local(
    queries, kv_cache, w_out, slot_page_before, slot_page_after, move_out, move_in, positions
):
    n = lax.axis_size("pages")
    cache_after = migrate_pages(kv_cache, slot_page_after, move_out, move_in)
    key_count = kv_cache.shape[0] * PAGE_TOK
    width = KV_HEADS * HEAD_DIM
    keys = kv_cache[:, :, 0, :].reshape(key_count, width)
    values_t = kv_cache[:, :, 1, :].reshape(key_count, KV_HEADS, HEAD_DIM).transpose(1, 2, 0)
    values_t = jnp.concatenate(
        [values_t, jnp.ones((KV_HEADS, SUM_ROWS, key_count), jnp.bfloat16)], axis=1
    )
    key_pos = (
        slot_page_before[:, None] * PAGE_TOK + jnp.arange(PAGE_TOK, dtype=jnp.int32)[None, :]
    ).reshape(key_count)
    live = jnp.repeat(slot_page_before >= 0, PAGE_TOK)
    visible = live[None, :, None] & (key_pos[None, :, None] <= positions[:, None, :])
    bias = jnp.where(visible, 0.0, floor_score).astype(jnp.float32)
    attended = attention(queries, keys, values_t, bias, n)
    return project(attended, w_out, n), cache_after


def solution(mesh):
    in_specs = (
        P(None, "groups", None),
        P(("groups", "pages"), None, None, None),
        P("pages", None),
        P(("groups", "pages")),
        P(("groups", "pages")),
        P(("groups", "pages"), None),
        P(("groups", "pages"), None),
        P(None, "groups"),
    )
    out_specs = (P(None, ("groups", "pages"), None), P(("groups", "pages"), None, None, None))
    return jax.shard_map(local, mesh=mesh, in_specs=in_specs, out_specs=out_specs, check_vma=False)
```

time: 827 us -> 253 us (0.31)
  waiting for transfers between devices: 273 us -> 0.01 us
  Pallas kernels: 0 us -> 196 us
  local copies, waits for them, and re-layouts: 203 us -> 30.5 us
  matrix products: 131 us -> 0 us
  blocking collectives: 75.4 us -> 0 us
  other arithmetic: 82.8 us -> 14.6 us
  starting transfers between devices: 37.8 us -> 7.26 us
  between operations: 15 us -> 3.35 us
    pallas_call x0 -> x2, Pallas kernels: none -> 196 us  [the longest x1 129 us: attention(): pl.pallas_call(functools.partial(attention_kernel, n, slots), out_shape=j...]
    all_to_all x6 -> x0, waiting for transfers between devices: 171 us -> none  [the longest x2 159 us: local(): lax.all_to_all(part_out.reshape(1, owners, tok_rows, D), 'pages', split_a...]
    dot_general x18 -> x0, matrix products: 131 us -> none  [the longest x8 71.5 us: one_block(): jnp.einsum('qhgk,khd->qhgd', weights, value_rows, preferred_element_type=...]
    reduce_scatter x2 -> x0, waiting for transfers between devices: 102 us -> none  [local(): lax.psum_scatter(jnp.dot(attended, w_out, preferred_element_type=jnp.floa...]
    all_to_all x2 -> x0, blocking collectives: 75.4 us -> none  [local(): lax.all_to_all(merged, 'pages', split_axis=1, concat_axis=0, tiled=True)]
    reduce_sum x12 -> x0, other arithmetic: 62.6 us -> none  [the longest x8 49 us: one_block(): row_sum = jnp.sum(weights, axis=-1, dtype=jnp.float32)]
    while x16 -> x0, local copies, waits for them, and re-layouts: 45.6 us -> none
    all_to_all x6 -> x0, starting transfers between devices: 31.8 us -> none  [the longest x2 11.2 us: local(): lax.all_to_all(part_max.reshape(1, owners, tok_rows, HEADS), 'pages', spl...]
  transfers between devices with their start and end apart: 12 -> 4, of which waited for: 4 -> 0; matrix products, arithmetic and copies ran while one was open for 44% -> 11% of each run, Pallas kernels for 0% -> 78%
where the time goes in v1:
time: 253 us; the launch traced here: 252 us
  Pallas kernels  196 us (77%)
  local copies, waits for them, and re-layouts  30.5 us (12%)
  other arithmetic  14.6 us (6%)
  starting transfers between devices  7.26 us (3%)
  between operations  3.35 us (1%)
    pallas_call x1, Pallas kernels, attention(): pl.pallas_call(functools.partial(attention_kernel, n, slots), out_shape=j...  129 us
    pallas_call x1, Pallas kernels, project(): pl.pallas_call(functools.partial(project_kernel, n, width), out_shape=jax...  67.5 us
    slice x1, local copies, waits for them, and re-layouts, local(): kv_cache[:, :, 1, :].reshape(key_count, KV_HEADS, HEAD_DIM)  14.3 us
    select_n x1, other arithmetic, migrate_pages(): arranged = jnp.where(landing, arrived[None], arranged)  10.3 us
    ppermute x4, starting transfers between devices, passed_along(): return lax.ppermute(block, axis, route)  7.26 us
  transfers between devices with their start and end apart: 4, of which 0 were waited for; matrix products, arithmetic and copies ran while one was open for 11% of the time, Pallas kernels for 78%

profile of v1, /device:TPU:0, one launch (start us, length us, event | category | flops | bytes accessed | tf_op | source)
XLA Modules:
  0.0 252.0 jit_solution(12358416830137182827)
XLA Ops:
  0.6 0.0 copy-start
  0.6 1.5 fusion
  4.7 4.1 %dynamic-slice_bitcast_fusion.3 = (bf16[128,2,1024]{2,1,0:T(2,128)(2,1)}, bf16[128,2,1024]{2,1,0:T(2,128)(2,1)}, bf16[128,2,1024]{2,1,0:T(2,128)(2,1)}, bf16[128,2,1024]{2,1,0:T(2,128)(2,1)}) fusion(bf16[8,128,2,1024]{3,2,1,0:T(2,128)(2,1)} %param.9, s32[]{:T(128)} %bitcast.5, s32[]{:T(128)} %bitcast.11, s32[]{:T(128)} %bitcast.8, s32[]{:T(128)} %bitcast.14), kind=kLoop, calls=%fused_computation.10 | loop fusion | bytes 4194320 | tf_op jit(solution)/shard_map/jit(dynamic_index_in_dim)/squeeze | solution.py:301
  8.9 0.5 collective-permute-start.3
  9.3 2.6 %collective-permute-start.2 = (bf16[128,2,1024]{2,1,0:T(2,128)(2,1)}, bf16[128,2,1024]{2,1,0:T(2,128)(2,1)S(1)}, u32[]{:S(2)}, u32[]{:S(2)}) collective-permute-start(bf16[128,2,1024]{2,1,0:T(2,128)(2,1)} %get-tuple-element.3), channel_id=1, source_target_pairs={{14,0},{15,1},{0,2},{1,3},{2,4},{3,5},{4,6},{5,7},{6,8},{7,9},{8,1... | collective-permute-start | bytes 1572872 | tf_op jit(solution)/shard_map/ppermute | solution.py:292
  11.9 2.5 collective-permute-start.1
  14.4 0.0 copy-start.4
  14.4 1.7 collective-permute-start
  16.1 0.0 copy-done
  16.1 14.3 %slice_reduce_fusion = (bf16[8,128,1024]{2,1,0:T(8,128)(2,1)S(1)}, bf16[8,128,1,1024]{3,2,1,0:T(2,128)(2,1)S(1)}) fusion(bf16[8,128,2,1024]{3,2,1,0:T(2,128)(2,1)S(1)} %copy-done), kind=kLoop, calls=%fused_computation.5 | loop fusion | bytes 8388608 | tf_op jit(solution)/shard_map/slice | solution.py:318
  30.4 0.0 copy-done.4
  30.4 2.1 copy.14
  32.6 1.9 copy.15
  34.5 0.0 copy-start.3
  34.5 3.3 %copy.13 = bf16[1024,8,128]{0,2,1:T(8,128)(2,1)S(1)} copy(bf16[1024,8,128]{2,1,0:T(8,128)(2,1)} %bitcast.27) | data formatting | bytes 4194304 | tf_op jit(solution)/shard_map/reshape;squeeze | solution.py:318
  37.8 0.1 add_bitcast_fusion
  37.9 0.1 broadcast_bitcast_fusion
  37.9 1.7 concatenate.3.vt_ref
  39.6 0.0 copy-done.3
  39.6 1.8 and_select_fusion.bias_ref
  41.4 128.7 %shard_map.95.attended_ref = bf16[512,512]{1,0:T(8,128)(2,1)} custom-call(bf16[2,256,8192]{2,1,0:T(8,128)(2,1)} %q_ref.1, bf16[1024,1024]{1,0:T(8,128)(2,1)} %bitcast.28, bf16[8,144,1024]{2,1,0:T(8,128)(2,1)} %concatenate.3.vt_ref, f32[2,1024,256]{2,1,0:T(8,128)} %and_select_fusion.bias_ref), custom_call_target="tpu_custom_call" | custom-call | flops 17179869184 | bytes 12582912 | tf_op jit(solution)/shard_map/pallas_call | solution.py:240
  170.1 0.0 copy-start.2
  170.1 0.0 copy-start.5
  170.1 67.5 %shard_map.96 = bf16[2,16,8192]{2,1,0:T(8,128)(2,1)} custom-call(bf16[512,512]{1,0:T(8,128)(2,1)} %shard_map.95.attended_ref, bf16[512,8192]{1,0:T(8,128)(2,1)} %w_ref.1), custom_call_target="tpu_custom_call" | custom-call | flops 4294967296 | bytes 8388608 | tf_op jit(solution)/shard_map/pallas_call | solution.py:272
  237.7 0.0 copy-done.2
  237.7 0.7 fusion.1
  238.3 1.2 iota_compare_fusion.2
  239.5 1.3 iota_compare_fusion
  240.8 0.0 copy-done.5
  240.9 0.0 collective-permute-done.3
  240.9 0.0 collective-permute-done.2
  240.9 0.0 collective-permute-done.1
  240.9 0.0 collective-permute-done
  240.9 0.0 copy-start.1
  240.9 10.3 %broadcast_select_fusion.4 = bf16[8,128,2,1024]{3,2,1,0:T(2,128)(2,1)} fusion(pred[8]{0:T(512)(128)(4,1)S(1)} %get-tuple-element.19, pred[8]{0:T(512)(128)(4,1)S(1)} %get-tuple-element.18, pred[8]{0:T(512)(128)(4,1)S(1)} %get-tuple-element.17, pred[8]{0:T(512)(128)(4,1)S(1)} %get-tuple-element.16, bf16[8,128,2,1024]{3,2,1,0:T(2,128)(2,1)} %param.9, ...), kind=kLoop, calls=%fused_computation.4 | loop fusion | flops 10485760 | bytes 10485800 | tf_op jit(solution)/shard_map/jit(_where)/select_n | solution.py:306
  251.2 0.0 copy-done.1
  251.2 0.8 copy.17
  (3 shorter events, 0.0 us)
Async XLA Ops:
  0.6 15.5 %copy-start = (bf16[8,128,2,1024]{3,2,1,0:T(2,128)(2,1)S(1)}, bf16[8,128,2,1024]{3,2,1,0:T(2,128)(2,1)}, u32[]{:S(2)}) copy-start(bf16[8,128,2,1024]{3,2,1,0:T(2,128)(2,1)} %param.9) | copy-start | bytes 12582916
  8.9 232.0 %collective-permute-start.3 = (bf16[128,2,1024]{2,1,0:T(2,128)(2,1)}, bf16[128,2,1024]{2,1,0:T(2,128)(2,1)S(1)}, u32[]{:S(2)}, u32[]{:S(2)}) collective-permute-start(bf16[128,2,1024]{2,1,0:T(2,128)(2,1)} %get-tuple-element.5), channel_id=1, source_target_pairs={{15,0},{0,1},{1,2},{2,3},{3,4},{4,5},{5,6},{6,7},{7,8},{8,9},{9,10... | collective-permute-start | bytes 1572872 | tf_op jit(solution)/shard_map/ppermute | solution.py:292
  9.3 231.6 %collective-permute-start.2 = (bf16[128,2,1024]{2,1,0:T(2,128)(2,1)}, bf16[128,2,1024]{2,1,0:T(2,128)(2,1)S(1)}, u32[]{:S(2)}, u32[]{:S(2)}) collective-permute-start(bf16[128,2,1024]{2,1,0:T(2,128)(2,1)} %get-tuple-element.3), channel_id=1, source_target_pairs={{14,0},{15,1},{0,2},{1,3},{2,4},{3,5},{4,6},{5,7},{6,8},{7,9},{8,1... | collective-permute-start | bytes 1572872 | tf_op jit(solution)/shard_map/ppermute | solution.py:292
  11.9 229.0 %collective-permute-start.1 = (bf16[128,2,1024]{2,1,0:T(2,128)(2,1)}, bf16[128,2,1024]{2,1,0:T(2,128)(2,1)}, u32[]{:S(2)}, u32[]{:S(2)}) collective-permute-start(bf16[128,2,1024]{2,1,0:T(2,128)(2,1)} %get-tuple-element.4), channel_id=1, source_target_pairs={{13,0},{14,1},{15,2},{0,3},{1,4},{2,5},{3,6},{4,7},{5,8},{6,9},{7,... | collective-permute-start | bytes 1572872 | tf_op jit(solution)/shard_map/ppermute | solution.py:292
  14.4 16.0 %copy-start.4 = (s32[8]{0:T(128)S(1)}, s32[8]{0:T(128)}, u32[]{:S(2)}) copy-start(s32[8]{0:T(128)} %param.11) | copy-start | bytes 100
  14.4 226.5 %collective-permute-start = (bf16[128,2,1024]{2,1,0:T(2,128)(2,1)}, bf16[128,2,1024]{2,1,0:T(2,128)(2,1)}, u32[]{:S(2)}, u32[]{:S(2)}) collective-permute-start(bf16[128,2,1024]{2,1,0:T(2,128)(2,1)} %get-tuple-element.2), channel_id=1, source_target_pairs={{12,0},{13,1},{14,2},{15,3},{0,4},{1,5},{2,6},{3,7},{4,8},{5,9},{6... | collective-permute-start | bytes 1572872 | tf_op jit(solution)/shard_map/ppermute | solution.py:292
  34.5 5.1 %copy-start.3 = (s32[2,256]{1,0:T(2,128)S(1)}, s32[2,256]{1,0:T(2,128)}, u32[]{:S(2)}) copy-start(s32[2,256]{1,0:T(2,128)} %param.15) | copy-start | bytes 6148
  170.1 67.5 %copy-start.2 = (s32[1,4]{1,0:T(1,128)S(1)}, s32[1,4]{1,0:T(1,128)}, u32[]{:S(2)}) copy-start(s32[1,4]{1,0:T(1,128)} %param.14) | copy-start | bytes 52
  170.1 70.7 %copy-start.5 = (s32[8]{0:T(128)S(1)}, s32[8]{0:T(128)}, u32[]{:S(2)}) copy-start(s32[8]{0:T(128)} %param.12) | copy-start | bytes 100
  240.9 10.3 %copy-start.1 = (bf16[2,16,8192]{2,1,0:T(8,128)(2,1)S(1)}, bf16[2,16,8192]{2,1,0:T(8,128)(2,1)}, u32[]{:S(2)}) copy-start(bf16[2,16,8192]{2,1,0:T(8,128)(2,1)} %shard_map.96) | copy-start | bytes 1572868

commit v2 on v1

--- a/solution.py
+++ b/solution.py
@@ -72,11 +72,12 @@
     keep, keep_l, send, send_l, recv, recv_l = (
         scratch[k * stages : (k + 1) * stages] for k in range(6)
     )
-    sems = scratch[6 * stages]
+    sems, sent_scores, kept_scores, top_ref = scratch[6 * stages :]
     me = lax.axis_index("pages")
     own_heads = HEADS // n
     tokens = q_ref.shape[1]
     chunks = 2 * own_heads
+    pairs = n // 2
     group = HEADS // KV_HEADS
     score_scale = HEAD_DIM ** (-0.5) * math.log2(math.e)
     greet_partners(me, stages)
@@ -91,37 +92,49 @@
         for copy in copies(s, i):
             copy.start()
 
+    mine = bit_of(me, 0)
+
+    def score(u, sent, buffer):
+        i, r = u // pairs, lax.rem(u, pairs)
+        block, j = i // own_heads, lax.rem(i, own_heads)
+        head = (2 * r + (1 - mine if sent else mine)) * own_heads + j
+        keys = k_ref[:, pl.ds(pl.multiple_of(head // group * HEAD_DIM, HEAD_DIM), HEAD_DIM)]
+        rows = q_ref[block, :, pl.ds(pl.multiple_of(head * HEAD_DIM, HEAD_DIM), HEAD_DIM)]
+        scores = lax.dot_general(
+            keys, rows, (((1,), (1,)), ((), ())), preferred_element_type=jnp.float32
+        )
+        scores = scores * score_scale + bias_ref[block]
+        buffer[...] = scores
+        return jnp.max(scores, axis=0, keepdims=True)
+
+    def mix(u, sent, buffer, top):
+        i, r = u // pairs, lax.rem(u, pairs)
+        head = (2 * r + (1 - mine if sent else mine)) * own_heads + lax.rem(i, own_heads)
+        weights = jnp.exp2(buffer[...] - top).astype(jnp.bfloat16)
+        mixed = jnp.dot(vt_ref[head // group], weights, preferred_element_type=jnp.float32)
+        total = mixed[HEAD_DIM : HEAD_DIM + 1]
+        mixed = mixed[:HEAD_DIM] * (1.0 / total)
+        level = top + jnp.log2(total)
+        if sent:
+            send[0][i, r] = mixed.astype(jnp.bfloat16)
+            send_l[0][i, pl.ds(r, 1)] = level
+        else:
+            slot = lax.rem(i, slots)
+            keep[0][slot, r] = mixed
+            keep_l[0][slot, pl.ds(r, 1)] = level
+
+    top_ref[...] = score(0, True, sent_scores)
+
     def produce(i):
-        block, j = i // own_heads, lax.rem(i, own_heads)
-        mine = bit_of(me, 0)
-        slot = lax.rem(i, slots)
-
-        def pair(r, carry):
-            for sent in (True, False):
-                owner = 2 * r + (1 - mine if sent else mine)
-                head = owner * own_heads + j
-                kv = head // group
-                keys = k_ref[:, pl.ds(pl.multiple_of(kv * HEAD_DIM, HEAD_DIM), HEAD_DIM)]
-                rows = q_ref[block, :, pl.ds(pl.multiple_of(head * HEAD_DIM, HEAD_DIM), HEAD_DIM)]
-                scores = lax.dot_general(
-                    keys, rows, (((1,), (1,)), ((), ())), preferred_element_type=jnp.float32
-                )
-                scores = scores * score_scale + bias_ref[block]
-                top = jnp.max(scores, axis=0, keepdims=True)
-                weights = jnp.exp2(scores - top).astype(jnp.bfloat16)
-                mixed = jnp.dot(vt_ref[kv], weights, preferred_element_type=jnp.float32)
-                total = mixed[HEAD_DIM : HEAD_DIM + 1]
-                mixed = mixed[:HEAD_DIM] / total
-                level = top + jnp.log2(total)
-                if sent:
-                    send[0][i, r] = mixed.astype(jnp.bfloat16)
-                    send_l[0][i, pl.ds(r, 1)] = level
-                else:
-                    keep[0][slot, r] = mixed
-                    keep_l[0][slot, pl.ds(r, 1)] = level
-            return carry
-
-        lax.fori_loop(0, n // 2, pair, 0)
+        def pair(r, top_sent):
+            u = i * pairs + r
+            top_kept = score(u, False, kept_scores)
+            mix(u, True, sent_scores, top_sent)
+            top_next = score(jnp.minimum(u + 1, chunks * pairs - 1), True, sent_scores)
+            mix(u, False, kept_scores, top_kept)
+            return top_next
+
+        top_ref[...] = lax.fori_loop(0, pairs, pair, top_ref[...])
 
     def merge(s, i):
         for copy in copies(s, i):
@@ -248,7 +261,9 @@
         + [pltpu.VMEM((chunks, p, tokens), jnp.float32) for p in rows]
         + [pltpu.VMEM((chunks, p, HEAD_DIM, tokens), jnp.bfloat16) for p in parts]
         + [pltpu.VMEM((chunks, p, tokens), jnp.float32) for p in rows]
-        + [pltpu.SemaphoreType.DMA((4, stages, chunks))],
+        + [pltpu.SemaphoreType.DMA((4, stages, chunks))]
+        + [pltpu.VMEM((key_count, tokens), jnp.float32)] * 2
+        + [pltpu.VMEM((1, tokens), jnp.float32)],
         compiler_params=pltpu.CompilerParams(
             collective_id=0, has_side_effects=True, vmem_limit_bytes=60 * 1024 * 1024
         ),
@@ -314,8 +329,17 @@
     cache_after = migrate_pages(kv_cache, slot_page_after, move_out, move_in)
     key_count = kv_cache.shape[0] * PAGE_TOK
     width = KV_HEADS * HEAD_DIM
-    keys = kv_cache[:, :, 0, :].reshape(key_count, width)
-    values_t = kv_cache[:, :, 1, :].reshape(key_count, KV_HEADS, HEAD_DIM).transpose(1, 2, 0)
+    pages = kv_cache.reshape(kv_cache.shape[0], 2 * PAGE_TOK, width)
+    pick = (
+        jnp.arange(2 * PAGE_TOK)[None, None, :]
+        == 2 * jnp.arange(PAGE_TOK)[None, :, None] + jnp.arange(2)[:, None, None]
+    ).astype(jnp.bfloat16)
+    keys = jnp.einsum(
+        "kr,srd->skd", pick[0], pages, preferred_element_type=jnp.bfloat16
+    ).reshape(key_count, width)
+    values_t = jnp.einsum(
+        "srd,kr->dsk", pages, pick[1], preferred_element_type=jnp.bfloat16
+    ).reshape(KV_HEADS, HEAD_DIM, key_count)
     values_t = jnp.concatenate(
         [values_t, jnp.ones((KV_HEADS, SUM_ROWS, key_count), jnp.bfloat16)], axis=1
     )

time: 253 us -> 215 us (0.85)
  Pallas kernels: 196 us -> 164 us
  local copies, waits for them, and re-layouts: 30.5 us -> 21.2 us
  matrix products: 0 us -> 5.13 us
    pallas_call x1, Pallas kernels: 129 us -> 96.5 us  [attention(): pl.pallas_call(functools.partial(attention_kernel, n, slots), out_shape=j...]
    slice x1 -> x0, local copies, waits for them, and re-layouts: 14.3 us -> none  [local(): kv_cache[:, :, 1, :].reshape(key_count, KV_HEADS, HEAD_DIM)]
    reshape x0 -> x2, local copies, waits for them, and re-layouts: none -> 10.4 us  [the longest x1 7.18 us: local(): pages = kv_cache.reshape(kv_cache.shape[0], 2 * PAGE_TOK, width)]
    dot_general x0 -> x2, matrix products: none -> 5.13 us  [the longest x1 4.41 us: local(): jnp.einsum('kr,srd->skd', pick[0], pages, preferred_element_type=jnp.bflo...]
    another operation x1 -> x0, local copies, waits for them, and re-layouts: 3.25 us -> none  [local(): kv_cache[:, :, 1, :].reshape(key_count, KV_HEADS, HEAD_DIM)]
  transfers between devices with their start and end apart: 4 -> 4, of which waited for: 0 -> 0; matrix products, arithmetic and copies ran while one was open for 11% -> 11% of each run, Pallas kernels for 78% -> 76%
where the time goes in v2:
time: 215 us
  Pallas kernels  164 us (76%)
  local copies, waits for them, and re-layouts  21.2 us (10%)
  other arithmetic  14.6 us (7%)
  starting transfers between devices  7.05 us (3%)
  matrix products  5.13 us (2%)
  between operations  3.28 us (2%)
    pallas_call x1, Pallas kernels, attention(): pl.pallas_call(functools.partial(attention_kernel, n, slots), out_shape=j...  96.5 us
    pallas_call x1, Pallas kernels, project(): pl.pallas_call(functools.partial(project_kernel, n, width), out_shape=jax...  67.1 us
    select_n x1, other arithmetic, migrate_pages(): arranged = jnp.where(landing, arrived[None], arranged)  10.3 us
    reshape x1, local copies, waits for them, and re-layouts, local(): pages = kv_cache.reshape(kv_cache.shape[0], 2 * PAGE_TOK, width)  7.18 us
    ppermute x4, starting transfers between devices, passed_along(): return lax.ppermute(block, axis, route)  7.05 us
    dot_general x1, matrix products, local(): jnp.einsum('kr,srd->skd', pick[0], pages, preferred_element_type=jnp.bflo...  4.41 us
  transfers between devices with their start and end apart: 4, of which 0 were waited for; matrix products, arithmetic and copies ran while one was open for 11% of the time, Pallas kernels for 76%

profile of v2, /device:TPU:0, one launch (start us, length us, event | category | flops | bytes accessed | tf_op | source)
XLA Modules:
  0.0 214.9 jit_solution(3479299827777392114)
XLA Ops:
  0.6 1.4 fusion.2
  4.5 4.2 %dynamic-slice_bitcast_fusion.3 = (bf16[128,2,1024]{2,1,0:T(2,128)(2,1)}, bf16[128,2,1024]{2,1,0:T(2,128)(2,1)}, bf16[128,2,1024]{2,1,0:T(2,128)(2,1)}, bf16[128,2,1024]{2,1,0:T(2,128)(2,1)}) fusion(bf16[8,128,2,1024]{3,2,1,0:T(2,128)(2,1)} %param.9, s32[]{:T(128)} %bitcast.10, s32[]{:T(128)} %bitcast.16, s32[]{:T(128)} %bitcast.13, s32[]{:T(128)} %bitcast.19), kind=kLoop, calls=%fused_computation.9 | loop fusion | bytes 4194320 | tf_op jit(solution)/shard_map/jit(dynamic_index_in_dim)/squeeze | solution.py:316
  8.7 0.4 collective-permute-start.3
  9.1 2.8 %collective-permute-start.2 = (bf16[128,2,1024]{2,1,0:T(2,128)(2,1)}, bf16[128,2,1024]{2,1,0:T(2,128)(2,1)S(1)}, u32[]{:S(2)}, u32[]{:S(2)}) collective-permute-start(bf16[128,2,1024]{2,1,0:T(2,128)(2,1)} %get-tuple-element.3), channel_id=1, source_target_pairs={{14,0},{15,1},{0,2},{1,3},{2,4},{3,5},{4,6},{5,7},{6,8},{7,9},{8,1... | collective-permute-start | bytes 1572872 | tf_op jit(solution)/shard_map/ppermute | solution.py:307
  11.9 2.2 %collective-permute-start.1 = (bf16[128,2,1024]{2,1,0:T(2,128)(2,1)}, bf16[128,2,1024]{2,1,0:T(2,128)(2,1)}, u32[]{:S(2)}, u32[]{:S(2)}) collective-permute-start(bf16[128,2,1024]{2,1,0:T(2,128)(2,1)} %get-tuple-element.4), channel_id=1, source_target_pairs={{13,0},{14,1},{15,2},{0,3},{1,4},{2,5},{3,6},{4,7},{5,8},{6,9},{7,... | collective-permute-start | bytes 1572872 | tf_op jit(solution)/shard_map/ppermute | solution.py:307
  14.1 1.6 collective-permute-start
  15.8 7.2 %reshape.88 = bf16[8,256,1024]{2,1,0:T(8,128)(2,1)} reshape(bf16[8,128,2,1024]{3,2,1,0:T(2,128)(2,1)} %param.9) | data formatting | bytes 8388608 | tf_op jit(solution)/shard_map/reshape | solution.py:332
  22.9 0.0 copy-start
  23.0 0.1 iota_compare_fusion
  23.1 4.4 %fusion.1 = bf16[128,8,1024]{2,0,1:T(8,128)(2,1)} fusion(bf16[8,256,1024]{2,1,0:T(8,128)(2,1)} %reshape.88, pred[2,128,256]{2,1,0:T(32,128)(4,1)S(1)} %iota_compare_fusion), kind=kOutput, calls=%fused_computation.14 | convolution fusion | flops 536870912 | bytes 6324224 | tf_op jit(solution)/shard_map/kr,srd->skd/dot_general | solution.py:337
  27.5 0.0 copy-done
  27.5 0.0 copy-start.4
  27.5 0.7 fusion
  28.2 0.0 copy-done.4
  28.2 1.9 copy.12
  30.2 0.0 copy-start.3
  30.2 3.3 %copy.11 = bf16[8,128,1024]{2,1,0:T(8,128)(2,1)S(1)} copy(bf16[8,128,1024]{1,0,2:T(8,128)(2,1)} %bitcast.40) | data formatting | bytes 4194304 | tf_op jit(solution)/shard_map/reshape | solution.py:342
  33.5 0.1 add_bitcast_fusion
  33.5 0.1 broadcast_bitcast_fusion
  33.6 1.7 concatenate.3.vt_ref
  35.3 0.0 copy-done.3
  35.3 1.8 and_select_fusion.bias_ref
  37.1 96.5 %shard_map.95.attended_ref = bf16[512,512]{1,0:T(8,128)(2,1)} custom-call(bf16[2,256,8192]{2,1,0:T(8,128)(2,1)} %q_ref.1, bf16[1024,1024]{1,0:T(8,128)(2,1)} %bitcast.41, bf16[8,144,1024]{2,1,0:T(8,128)(2,1)} %concatenate.3.vt_ref, f32[2,1024,256]{2,1,0:T(8,128)} %and_select_fusion.bias_ref), custom_call_target="tpu_custom_call" | custom-call | flops 17179869184 | bytes 12582912 | tf_op jit(solution)/shard_map/pallas_call | solution.py:253
  133.6 0.0 copy-start.2
  133.6 0.0 copy-start.5
  133.6 67.1 %shard_map.96 = bf16[2,16,8192]{2,1,0:T(8,128)(2,1)} custom-call(bf16[512,512]{1,0:T(8,128)(2,1)} %shard_map.95.attended_ref, bf16[512,8192]{1,0:T(8,128)(2,1)} %w_ref.1), custom_call_target="tpu_custom_call" | custom-call | flops 4294967296 | bytes 8388608 | tf_op jit(solution)/shard_map/pallas_call | solution.py:287
  200.7 0.0 copy-done.2
  200.7 0.7 fusion.3
  201.4 1.2 iota_compare_fusion.3
  202.5 1.2 iota_compare_fusion.1
  203.8 0.0 copy-done.5
  203.8 0.0 collective-permute-done.3
  203.8 0.0 collective-permute-done.2
  203.8 0.0 collective-permute-done.1
  203.8 0.0 collective-permute-done
  203.8 0.0 copy-start.1
  203.8 10.3 %broadcast_select_fusion.4 = bf16[8,128,2,1024]{3,2,1,0:T(2,128)(2,1)} fusion(pred[8]{0:T(512)(128)(4,1)S(1)} %get-tuple-element.17, pred[8]{0:T(512)(128)(4,1)S(1)} %get-tuple-element.16, pred[8]{0:T(512)(128)(4,1)S(1)} %get-tuple-element.15, pred[8]{0:T(512)(128)(4,1)S(1)} %get-tuple-element.14, bf16[8,128,2,1024]{3,2,1,0:T(2,128)(2,1)} %param.9, ...), kind=kLoop, calls=%fused_computation.4 | loop fusion | flops 10485760 | bytes 10485800 | tf_op jit(solution)/shard_map/jit(_where)/select_n | solution.py:321
  214.1 0.0 copy-done.1
  214.1 0.8 copy.15
  (5 shorter events, 0.0 us)
Async XLA Ops:
  8.7 195.1 %collective-permute-start.3 = (bf16[128,2,1024]{2,1,0:T(2,128)(2,1)}, bf16[128,2,1024]{2,1,0:T(2,128)(2,1)S(1)}, u32[]{:S(2)}, u32[]{:S(2)}) collective-permute-start(bf16[128,2,1024]{2,1,0:T(2,128)(2,1)} %get-tuple-element.5), channel_id=1, source_target_pairs={{15,0},{0,1},{1,2},{2,3},{3,4},{4,5},{5,6},{6,7},{7,8},{8,9},{9,10... | collective-permute-start | bytes 1572872 | tf_op jit(solution)/shard_map/ppermute | solution.py:307
  9.1 194.7 %collective-permute-start.2 = (bf16[128,2,1024]{2,1,0:T(2,128)(2,1)}, bf16[128,2,1024]{2,1,0:T(2,128)(2,1)S(1)}, u32[]{:S(2)}, u32[]{:S(2)}) collective-permute-start(bf16[128,2,1024]{2,1,0:T(2,128)(2,1)} %get-tuple-element.3), channel_id=1, source_target_pairs={{14,0},{15,1},{0,2},{1,3},{2,4},{3,5},{4,6},{5,7},{6,8},{7,9},{8,1... | collective-permute-start | bytes 1572872 | tf_op jit(solution)/shard_map/ppermute | solution.py:307
  11.9 191.9 %collective-permute-start.1 = (bf16[128,2,1024]{2,1,0:T(2,128)(2,1)}, bf16[128,2,1024]{2,1,0:T(2,128)(2,1)}, u32[]{:S(2)}, u32[]{:S(2)}) collective-permute-start(bf16[128,2,1024]{2,1,0:T(2,128)(2,1)} %get-tuple-element.4), channel_id=1, source_target_pairs={{13,0},{14,1},{15,2},{0,3},{1,4},{2,5},{3,6},{4,7},{5,8},{6,9},{7,... | collective-permute-start | bytes 1572872 | tf_op jit(solution)/shard_map/ppermute | solution.py:307
  14.1 189.7 %collective-permute-start = (bf16[128,2,1024]{2,1,0:T(2,128)(2,1)}, bf16[128,2,1024]{2,1,0:T(2,128)(2,1)}, u32[]{:S(2)}, u32[]{:S(2)}) collective-permute-start(bf16[128,2,1024]{2,1,0:T(2,128)(2,1)} %get-tuple-element.2), channel_id=1, source_target_pairs={{12,0},{13,1},{14,2},{15,3},{0,4},{1,5},{2,6},{3,7},{4,8},{5,9},{6... | collective-permute-start | bytes 1572872 | tf_op jit(solution)/shard_map/ppermute | solution.py:307
  22.9 4.5 %copy-start = (bf16[8,256,1024]{2,1,0:T(8,128)(2,1)S(1)}, bf16[8,256,1024]{2,1,0:T(8,128)(2,1)}, u32[]{:S(2)}) copy-start(bf16[8,256,1024]{2,1,0:T(8,128)(2,1)} %reshape.88) | copy-start | bytes 12582916
  27.5 0.7 copy-start.4
  30.2 5.1 %copy-start.3 = (s32[2,256]{1,0:T(2,128)S(1)}, s32[2,256]{1,0:T(2,128)}, u32[]{:S(2)}) copy-start(s32[2,256]{1,0:T(2,128)} %param.15) | copy-start | bytes 6148
  133.6 67.1 %copy-start.2 = (s32[1,4]{1,0:T(1,128)S(1)}, s32[1,4]{1,0:T(1,128)}, u32[]{:S(2)}) copy-start(s32[1,4]{1,0:T(1,128)} %param.14) | copy-start | bytes 52
  133.6 70.2 %copy-start.5 = (s32[8]{0:T(128)S(1)}, s32[8]{0:T(128)}, u32[]{:S(2)}) copy-start(s32[8]{0:T(128)} %param.12) | copy-start | bytes 100
  203.8 10.3 %copy-start.1 = (bf16[2,16,8192]{2,1,0:T(8,128)(2,1)S(1)}, bf16[2,16,8192]{2,1,0:T(8,128)(2,1)}, u32[]{:S(2)}) copy-start(bf16[2,16,8192]{2,1,0:T(8,128)(2,1)} %shard_map.96) | copy-start | bytes 1572868

commit v3 on v2

--- a/solution.py
+++ b/solution.py
@@ -134,7 +134,7 @@
             mix(u, False, kept_scores, top_kept)
             return top_next
 
-        top_ref[...] = lax.fori_loop(0, pairs, pair, top_ref[...])
+        top_ref[...] = lax.fori_loop(0, pairs, pair, top_ref[...], unroll=2)
 
     def merge(s, i):
         for copy in copies(s, i):

time: 215 us -> 207 us (0.963)
  Pallas kernels: 164 us -> 155 us
    pallas_call x1, Pallas kernels: 96.5 us -> 90.8 us  [attention(): pl.pallas_call(functools.partial(attention_kernel, n, slots), out_shape=j...]
    pallas_call x1, Pallas kernels: 67.1 us -> 64.6 us  [project(): pl.pallas_call(functools.partial(project_kernel, n, width), out_shape=jax...]
  transfers between devices with their start and end apart: 4 -> 4, of which waited for: 0 -> 0; matrix products, arithmetic and copies ran while one was open for 11% -> 12% of each run, Pallas kernels for 76% -> 75%
where the time goes in v3:
time: 207 us
  Pallas kernels  155 us (75%)
  local copies, waits for them, and re-layouts  21.4 us (10%)
  other arithmetic  14.6 us (7%)
  starting transfers between devices  6.81 us (3%)
  matrix products  5.13 us (2%)
  between operations  3.28 us (2%)
    pallas_call x1, Pallas kernels, attention(): pl.pallas_call(functools.partial(attention_kernel, n, slots), out_shape=j...  90.8 us
    pallas_call x1, Pallas kernels, project(): pl.pallas_call(functools.partial(project_kernel, n, width), out_shape=jax...  64.6 us
    select_n x1, other arithmetic, migrate_pages(): arranged = jnp.where(landing, arrived[None], arranged)  10.3 us
    reshape x1, local copies, waits for them, and re-layouts, local(): pages = kv_cache.reshape(kv_cache.shape[0], 2 * PAGE_TOK, width)  7.18 us
    ppermute x4, starting transfers between devices, passed_along(): return lax.ppermute(block, axis, route)  6.81 us
    dot_general x1, matrix products, local(): jnp.einsum('kr,srd->skd', pick[0], pages, preferred_element_type=jnp.bflo...  4.4 us
    squeeze x1, local copies, waits for them, and re-layouts, migrate_pages(): lax.dynamic_index_in_dim(kv_cache, jnp.maximum(move_out[0, offset - 1], 0...  4.38 us
  transfers between devices with their start and end apart: 4, of which 0 were waited for; matrix products, arithmetic and copies ran while one was open for 12% of the time, Pallas kernels for 75%

profile of v3, /device:TPU:0, one launch (start us, length us, event | category | flops | bytes accessed | tf_op | source)
XLA Modules:
  0.0 206.7 jit_solution(756234669730537787)
XLA Ops:
  0.6 1.4 fusion.2
  4.5 4.4 %dynamic-slice_bitcast_fusion.3 = (bf16[128,2,1024]{2,1,0:T(2,128)(2,1)}, bf16[128,2,1024]{2,1,0:T(2,128)(2,1)}, bf16[128,2,1024]{2,1,0:T(2,128)(2,1)}, bf16[128,2,1024]{2,1,0:T(2,128)(2,1)}) fusion(bf16[8,128,2,1024]{3,2,1,0:T(2,128)(2,1)} %param.9, s32[]{:T(128)} %bitcast.10, s32[]{:T(128)} %bitcast.16, s32[]{:T(128)} %bitcast.13, s32[]{:T(128)} %bitcast.19), kind=kLoop, calls=%fused_computation.9 | loop fusion | bytes 4194320 | tf_op jit(solution)/shard_map/jit(dynamic_index_in_dim)/squeeze | solution.py:316
  8.9 0.5 collective-permute-start.3
  9.4 2.3 %collective-permute-start.2 = (bf16[128,2,1024]{2,1,0:T(2,128)(2,1)}, bf16[128,2,1024]{2,1,0:T(2,128)(2,1)S(1)}, u32[]{:S(2)}, u32[]{:S(2)}) collective-permute-start(bf16[128,2,1024]{2,1,0:T(2,128)(2,1)} %get-tuple-element.3), channel_id=1, source_target_pairs={{14,0},{15,1},{0,2},{1,3},{2,4},{3,5},{4,6},{5,7},{6,8},{7,9},{8,1... | collective-permute-start | bytes 1572872 | tf_op jit(solution)/shard_map/ppermute | solution.py:307
  11.7 2.4 %collective-permute-start.1 = (bf16[128,2,1024]{2,1,0:T(2,128)(2,1)}, bf16[128,2,1024]{2,1,0:T(2,128)(2,1)}, u32[]{:S(2)}, u32[]{:S(2)}) collective-permute-start(bf16[128,2,1024]{2,1,0:T(2,128)(2,1)} %get-tuple-element.4), channel_id=1, source_target_pairs={{13,0},{14,1},{15,2},{0,3},{1,4},{2,5},{3,6},{4,7},{5,8},{6,9},{7,... | collective-permute-start | bytes 1572872 | tf_op jit(solution)/shard_map/ppermute | solution.py:307
  14.1 1.6 collective-permute-start
  15.7 7.2 %reshape.88 = bf16[8,256,1024]{2,1,0:T(8,128)(2,1)} reshape(bf16[8,128,2,1024]{3,2,1,0:T(2,128)(2,1)} %param.9) | data formatting | bytes 8388608 | tf_op jit(solution)/shard_map/reshape | solution.py:332
  22.9 0.0 copy-start
  22.9 0.1 iota_compare_fusion
  23.0 4.4 %fusion.1 = bf16[128,8,1024]{2,0,1:T(8,128)(2,1)} fusion(bf16[8,256,1024]{2,1,0:T(8,128)(2,1)} %reshape.88, pred[2,128,256]{2,1,0:T(32,128)(4,1)S(1)} %iota_compare_fusion), kind=kOutput, calls=%fused_computation.14 | convolution fusion | flops 536870912 | bytes 6324224 | tf_op jit(solution)/shard_map/kr,srd->skd/dot_general | solution.py:337
  27.4 0.0 copy-done
  27.4 0.0 copy-start.4
  27.4 0.7 fusion
  28.2 0.0 copy-done.4
  28.2 1.9 copy.12
  30.1 0.0 copy-start.3
  30.1 3.3 %copy.11 = bf16[8,128,1024]{2,1,0:T(8,128)(2,1)S(1)} copy(bf16[8,128,1024]{1,0,2:T(8,128)(2,1)} %bitcast.40) | data formatting | bytes 4194304 | tf_op jit(solution)/shard_map/reshape | solution.py:342
  33.4 0.1 add_bitcast_fusion
  33.5 0.1 broadcast_bitcast_fusion
  33.6 1.7 concatenate.3.vt_ref
  35.3 0.0 copy-done.3
  35.3 1.8 and_select_fusion.bias_ref
  37.0 90.8 %shard_map.95.attended_ref = bf16[512,512]{1,0:T(8,128)(2,1)} custom-call(bf16[2,256,8192]{2,1,0:T(8,128)(2,1)} %q_ref.1, bf16[1024,1024]{1,0:T(8,128)(2,1)} %bitcast.41, bf16[8,144,1024]{2,1,0:T(8,128)(2,1)} %concatenate.3.vt_ref, f32[2,1024,256]{2,1,0:T(8,128)} %and_select_fusion.bias_ref), custom_call_target="tpu_custom_call" | custom-call | flops 17179869184 | bytes 12582912 | tf_op jit(solution)/shard_map/pallas_call | solution.py:253
  127.9 0.0 copy-start.2
  127.9 0.0 copy-start.5
  127.9 64.6 %shard_map.96 = bf16[2,16,8192]{2,1,0:T(8,128)(2,1)} custom-call(bf16[512,512]{1,0:T(8,128)(2,1)} %shard_map.95.attended_ref, bf16[512,8192]{1,0:T(8,128)(2,1)} %w_ref.1), custom_call_target="tpu_custom_call" | custom-call | flops 4294967296 | bytes 8388608 | tf_op jit(solution)/shard_map/pallas_call | solution.py:287
  192.5 0.0 copy-done.2
  192.5 0.7 fusion.3
  193.1 1.2 iota_compare_fusion.3
  194.3 1.2 iota_compare_fusion.1
  195.5 0.0 copy-done.5
  195.6 0.0 collective-permute-done.3
  195.6 0.0 collective-permute-done.2
  195.6 0.0 collective-permute-done.1
  195.6 0.0 collective-permute-done
  195.6 0.0 copy-start.1
  195.6 10.3 %broadcast_select_fusion.4 = bf16[8,128,2,1024]{3,2,1,0:T(2,128)(2,1)} fusion(pred[8]{0:T(512)(128)(4,1)S(1)} %get-tuple-element.17, pred[8]{0:T(512)(128)(4,1)S(1)} %get-tuple-element.16, pred[8]{0:T(512)(128)(4,1)S(1)} %get-tuple-element.15, pred[8]{0:T(512)(128)(4,1)S(1)} %get-tuple-element.14, bf16[8,128,2,1024]{3,2,1,0:T(2,128)(2,1)} %param.9, ...), kind=kLoop, calls=%fused_computation.4 | loop fusion | flops 10485760 | bytes 10485800 | tf_op jit(solution)/shard_map/jit(_where)/select_n | solution.py:321
  205.9 0.0 copy-done.1
  205.9 0.8 copy.15
  (5 shorter events, 0.0 us)
Async XLA Ops:
  8.9 186.6 %collective-permute-start.3 = (bf16[128,2,1024]{2,1,0:T(2,128)(2,1)}, bf16[128,2,1024]{2,1,0:T(2,128)(2,1)S(1)}, u32[]{:S(2)}, u32[]{:S(2)}) collective-permute-start(bf16[128,2,1024]{2,1,0:T(2,128)(2,1)} %get-tuple-element.5), channel_id=1, source_target_pairs={{15,0},{0,1},{1,2},{2,3},{3,4},{4,5},{5,6},{6,7},{7,8},{8,9},{9,10... | collective-permute-start | bytes 1572872 | tf_op jit(solution)/shard_map/ppermute | solution.py:307
  9.4 186.2 %collective-permute-start.2 = (bf16[128,2,1024]{2,1,0:T(2,128)(2,1)}, bf16[128,2,1024]{2,1,0:T(2,128)(2,1)S(1)}, u32[]{:S(2)}, u32[]{:S(2)}) collective-permute-start(bf16[128,2,1024]{2,1,0:T(2,128)(2,1)} %get-tuple-element.3), channel_id=1, source_target_pairs={{14,0},{15,1},{0,2},{1,3},{2,4},{3,5},{4,6},{5,7},{6,8},{7,9},{8,1... | collective-permute-start | bytes 1572872 | tf_op jit(solution)/shard_map/ppermute | solution.py:307
  11.7 183.9 %collective-permute-start.1 = (bf16[128,2,1024]{2,1,0:T(2,128)(2,1)}, bf16[128,2,1024]{2,1,0:T(2,128)(2,1)}, u32[]{:S(2)}, u32[]{:S(2)}) collective-permute-start(bf16[128,2,1024]{2,1,0:T(2,128)(2,1)} %get-tuple-element.4), channel_id=1, source_target_pairs={{13,0},{14,1},{15,2},{0,3},{1,4},{2,5},{3,6},{4,7},{5,8},{6,9},{7,... | collective-permute-start | bytes 1572872 | tf_op jit(solution)/shard_map/ppermute | solution.py:307
  14.1 181.5 %collective-permute-start = (bf16[128,2,1024]{2,1,0:T(2,128)(2,1)}, bf16[128,2,1024]{2,1,0:T(2,128)(2,1)}, u32[]{:S(2)}, u32[]{:S(2)}) collective-permute-start(bf16[128,2,1024]{2,1,0:T(2,128)(2,1)} %get-tuple-element.2), channel_id=1, source_target_pairs={{12,0},{13,1},{14,2},{15,3},{0,4},{1,5},{2,6},{3,7},{4,8},{5,9},{6... | collective-permute-start | bytes 1572872 | tf_op jit(solution)/shard_map/ppermute | solution.py:307
  22.9 4.5 %copy-start = (bf16[8,256,1024]{2,1,0:T(8,128)(2,1)S(1)}, bf16[8,256,1024]{2,1,0:T(8,128)(2,1)}, u32[]{:S(2)}) copy-start(bf16[8,256,1024]{2,1,0:T(8,128)(2,1)} %reshape.88) | copy-start | bytes 12582916
  27.4 0.7 copy-start.4
  30.1 5.1 %copy-start.3 = (s32[2,256]{1,0:T(2,128)S(1)}, s32[2,256]{1,0:T(2,128)}, u32[]{:S(2)}) copy-start(s32[2,256]{1,0:T(2,128)} %param.15) | copy-start | bytes 6148
  127.9 64.6 %copy-start.2 = (s32[1,4]{1,0:T(1,128)S(1)}, s32[1,4]{1,0:T(1,128)}, u32[]{:S(2)}) copy-start(s32[1,4]{1,0:T(1,128)} %param.14) | copy-start | bytes 52
  127.9 67.7 %copy-start.5 = (s32[8]{0:T(128)S(1)}, s32[8]{0:T(128)}, u32[]{:S(2)}) copy-start(s32[8]{0:T(128)} %param.12) | copy-start | bytes 100
  195.6 10.3 %copy-start.1 = (bf16[2,16,8192]{2,1,0:T(8,128)(2,1)S(1)}, bf16[2,16,8192]{2,1,0:T(8,128)(2,1)}, u32[]{:S(2)}) copy-start(bf16[2,16,8192]{2,1,0:T(8,128)(2,1)} %shard_map.96) | copy-start | bytes 1572868
